TPU v7x, 32 devices: a whole 2x2x4 slice. The times are simulated.
32 devices in a mesh: groups: 2 (over y), blocks: 4 (over z), views: 2 (over x), sub: 2 (over core).
Axes of the slice: x: 2, y: 2, z: 4, core: 2. Of those that a mesh axis runs over, the one named last changes fastest.
Arguments:
- estimate0: float32 [128, 32, 512], P(('groups', 'blocks'), 'sub', 'views'), parts along dimension 0, may hold values from 0.25 to 4
- measured: bfloat16 [8, 2, 2048, 512], P('views', 'sub', ('groups', 'blocks')), parts along dimension 2, may hold values from 0.19921875 to 5
- line_target: int32 [8, 2, 2048], P('views', 'sub', ('groups', 'blocks')), parts along dimension 2, may hold values from 0 to 1023, as said below
- band: int32 [8, 64], replicated, may hold values from 0 to 7
- psf: float32 [8, 8, 17], replicated, may hold values from 0.02 to 0.12
- background: float32 [8], replicated, may hold values from 0.1 to 1
Outputs:
- estimate: float32 [128, 32, 512], P(('groups', 'blocks'), 'sub', 'views'), parts along dimension 0
There are 2 independent parts, one for each index of `groups`. A program takes and returns all parts, laid end to end along the dimension named above; an argument that names none is the same for every part. Nothing has to cross between parts.
Inputs may be any that keep to these rules, and one draw needn't show every extreme that they name: For each view v and y range h, line_target[v, h] is a permutation of 0 .. 1023. The lines held by one device (aligned runs of 256 lines) send at most 128 lines to any one z-block, and this most is reached by every device.
All inputs are finite; a program needn't handle non-finite values.
Results may differ from a plain program's by a relative error of at most 0.0003.
Values may be sent and summed in bfloat16 or wider, within the bound.
A program may use at most 64 MiB of HBM per device.

v0:
```python
import jax
import jax.numpy as jnp
from jax import lax
from jax.sharding import PartitionSpec as P

ITERS = 2


def padded(array, sides, width):
    for axis, dim in sides:
        size, length = (lax.axis_size(axis), array.shape[dim])
        up = [(i, (i + 1) % size) for i in range(size - 1)]
        down = [(j, i) for i, j in up]
        last = lax.slice_in_dim(array, length - width, length, axis=dim)
        leading = lax.slice_in_dim(array, 0, width, axis=dim)
        before = lax.ppermute(last, axis, up)
        after = lax.ppermute(leading, axis, down)
        array = jnp.concatenate([before, array, after], axis=dim)
    return array


def shards(estimate0, measured, line_target, band, psf, background):
    n_blocks = lax.axis_size("blocks")
    n_views = lax.axis_size("views")
    view_count = measured.shape[0]
    depth_count = estimate0.shape[0]
    row_count = estimate0.shape[1]
    x_local = estimate0.shape[2]
    line_count = line_target.shape[2]
    full_width = measured.shape[3]
    tap_count = psf.shape[2]
    all_views = psf.shape[0]
    half_width = (tap_count - 1) // 2
    window_len = depth_count + 2 * half_width
    slab_depth = band.shape[1]
    start_z = lax.axis_index("blocks") * depth_count
    highest = lax.Precision.HIGHEST
    targets = line_target[:, 0, :]
    destination = targets // line_count
    local_line = targets % line_count
    capacity = 2 * line_count // n_blocks
    onehot = (
        destination[:, :, None] == jnp.arange(n_blocks, dtype=jnp.int32)[None, None, :]
    ).astype(jnp.int32)
    running = jnp.cumsum(onehot, axis=1)
    slot_index = jnp.sum(onehot * running, axis=2) - 1
    position = destination * capacity + slot_index
    view_rows = jnp.arange(view_count, dtype=jnp.int32)[:, None]
    send_rows = (
        jnp.zeros((view_count, n_blocks * capacity, full_width), measured.dtype)
        .at[view_rows, position]
        .set(measured[:, 0])
    )
    send_ids = (
        jnp.full((view_count, n_blocks * capacity), -1, jnp.int32)
        .at[view_rows, position]
        .set(local_line)
    )
    offsets = jnp.arange(window_len, dtype=jnp.int32) + start_z - half_width
    valid = ((offsets >= 0) & (offsets < slab_depth)).astype(jnp.float32)
    padded_band = jnp.pad(band, ((0, 0), (half_width, half_width)), mode="edge")
    band_window = lax.dynamic_slice_in_dim(padded_band, start_z, window_len, 1)
    band_onehot = (
        band_window[:, :, None] == jnp.arange(psf.shape[1], dtype=jnp.int32)[None, None, :]
    ).astype(jnp.float32)
    coef_all = (
        jnp.einsum("vwb,vbk->vwk", band_onehot, psf, precision=highest) * valid[None, :, None]
    )
    z_local = jnp.arange(depth_count, dtype=jnp.int32)
    w_index = jnp.arange(window_len, dtype=jnp.int32)
    k_index = jnp.arange(tap_count, dtype=jnp.int32)
    forward_pick = (
        w_index[None, :, None] - z_local[:, None, None] == k_index[None, None, :]
    ).astype(jnp.float32)
    backward_pick = (
        z_local[None, :, None] - w_index[:, None, None] + 2 * half_width == k_index[None, None, :]
    ).astype(jnp.float32)
    norm_sum = jnp.einsum("vwk,wck->c", coef_all, backward_pick, precision=highest)
    estimate = estimate0
    rows_four = send_rows.reshape(view_count, n_blocks, capacity, full_width)
    ids_four = jnp.broadcast_to(
        send_ids.reshape(view_count, n_blocks, capacity)[:, :, :, None],
        (view_count, n_blocks, capacity, n_views),
    )
    recv_rows, recv_ids = (
        lax.all_to_all(
            lax.all_to_all(rows_four, "blocks", split_axis=1, concat_axis=1, tiled=True),
            "views",
            split_axis=3,
            concat_axis=0,
            tiled=True,
        ),
        lax.all_to_all(
            lax.all_to_all(ids_four, "blocks", split_axis=1, concat_axis=1, tiled=True),
            "views",
            split_axis=3,
            concat_axis=0,
            tiled=True,
        ),
    )
    recv_ids = recv_ids[:, :, :, 0].reshape(all_views, n_blocks * capacity)
    place = jnp.where(recv_ids < 0, line_count, recv_ids)
    every_view = jnp.arange(all_views, dtype=jnp.int32)[:, None]
    observed = (
        jnp.zeros((all_views, line_count, x_local), measured.dtype)
        .at[every_view, place]
        .set(recv_rows.reshape(all_views, n_blocks * capacity, x_local), mode="drop")
    )
    observed = observed.reshape(all_views, depth_count, row_count, x_local)
    forward_all = jnp.einsum(
        "vzk,zwk->vzw",
        coef_all[:, half_width : half_width + depth_count],
        forward_pick,
        precision=highest,
    )
    for sweep in range(ITERS):
        extended = padded(estimate, (("blocks", 0),), half_width)
        forward = (
            jnp.einsum("vzw,wyx->vzyx", forward_all, extended, precision=highest)
            + background[:, None, None, None]
        )
        ratio = observed.astype(jnp.float32) / forward
        spread = jnp.einsum("vzw,vzyx->wyx", forward_all, ratio, precision=highest)
        outward = jnp.concatenate([spread[:half_width], spread[half_width + depth_count :]], axis=0)
        inward = padded(outward, (("blocks", 0),), half_width)
        share = spread[half_width : half_width + depth_count]
        share = share.at[:half_width].add(inward[:half_width])
        share = share.at[depth_count - half_width :].add(inward[3 * half_width :])
        estimate = estimate * share / norm_sum[:, None, None]
    return estimate


def solution(mesh):
    in_specs = (
        P(("groups", "blocks"), "sub", "views"),
        P("views", "sub", ("groups", "blocks"), None),
        P("views", "sub", ("groups", "blocks")),
        P(),
        P(),
        P(),
    )
    out_specs = P(("groups", "blocks"), "sub", "views")
    return jax.shard_map(shards, mesh=mesh, in_specs=in_specs, out_specs=out_specs, check_vma=False)
```

profile of v0, /device:TPU:0, one launch (start us, length us, event | category | flops | bytes accessed | tf_op | source)
XLA Modules:
  0.0 176.8 jit_solution(15169412571177774338)
XLA Ops:
  1.4 4.8 %reduce-window.6 = s32[4,4,2,128]{3,2,1,0:T(2,128)S(1)} reduce-window(s32[4,4,2,128]{3,2,1,0:T(2,128)S(1)} %compare_convert_fusion, s32[]{:T(128)} %constant.147.clone.1), window={size=1x1x1x128 pad=0_0x0_0x0_0x127_0}, to_apply=%region_0.1 | reduce-window | flops 520192 | bytes 32772 | tf_op jit(solution)/shard_map/reduce-window
  9.0 4.3 %scatter_custom_fusion = s32[2048]{0:T(1024)S(1)} fusion(s32[1024]{0:T(1024)S(1)} %bitcast.107, s32[1024]{0:T(1024)S(1)} %bitcast.109, s32[]{:T(128)} %constant.155.clone.1), kind=kCustom, calls=%fused_computation.86 | custom fusion | bytes 8196
  14.0 6.3 %all-to-all-start = ((s32[4,4,128,2]{2,0,3,1:T(4,128)}), s32[4,4,128,2]{2,0,3,1:T(4,128)S(1)}, u32[]{:S(2)}, u32[]{:S(2)}) async-start(s32[4,4,128,2]{2,0,3,1:T(4,128)} %broadcast_in_dim.26), calls=%async_computation | async-start | bytes 32768 | tf_op jit(solution)/shard_map/all_to_all | solution.py:94
  20.3 6.3 %scatter_custom_fusion.1 = bf16[2048,512]{1,0:T(8,128)(2,1)S(1)} fusion(s32[1024]{0:T(1024)S(1)} %bitcast.108, bf16[1024,512]{1,0:T(8,128)(2,1)} %bitcast.110, bf16[]{:T(256)} %constant.154.clone.1), kind=kCustom, calls=%fused_computation.14 | custom fusion | bytes 2097664
  26.6 1.6 copy.78
  28.1 5.2 %all-to-all-start.2 = ((bf16[4,4,128,512]{3,2,0,1:T(8,128)(2,1)}), bf16[4,4,128,512]{3,2,0,1:T(8,128)(2,1)S(1)}, u32[]{:S(2)}, u32[]{:S(2)}) async-start(bf16[4,4,128,512]{3,2,0,1:T(8,128)(2,1)} %copy.78), calls=%async_computation.2 | async-start | bytes 4194304 | tf_op jit(solution)/shard_map/all_to_all | solution.py:87
  33.5 3.9 %collective-permute-start = (f32[8,16,256]{2,0,1:T(8,128)S(1)}, f32[8,16,256]{2,0,1:T(8,128)S(1)}, u32[]{:S(2)}, u32[]{:S(2)}) collective-permute-start(f32[8,16,256]{2,0,1:T(8,128)S(1)} %get-tuple-element.61), channel_id=1, source_target_pairs={{0,4},{4,8},{8,12},{1,5},{5,9},{9,13},{2,6},{6,10},{10,14},{3,7},{... | collective-permute-start | bytes 393224 | tf_op jit(solution)/shard_map/ppermute | solution.py:16
  40.2 41.8 %all-to-all-done.2 = bf16[4,4,128,512]{3,2,0,1:T(8,128)(2,1)S(1)} async-done(((bf16[4,4,128,512]{3,2,0,1:T(8,128)(2,1)}), bf16[4,4,128,512]{3,2,0,1:T(8,128)(2,1)S(1)}, u32[]{:S(2)}, u32[]{:S(2)}) %all-to-all-start.2) | async-done | bytes 2097184 | tf_op jit(solution)/shard_map/all_to_all | solution.py:87
  82.0 3.2 %all-to-all-start.1 = ((s32[4,4,128,2]{2,0,1,3:T(4,128)}), s32[4,4,128,2]{2,0,1,3:T(4,128)S(1)}, u32[]{:S(2)}, u32[]{:S(2)}) async-start(s32[4,4,128,2]{2,0,1,3:T(4,128)} %copy.76), calls=%async_computation.1 | async-start | bytes 32768 | tf_op jit(solution)/shard_map/all_to_all | solution.py:93
  85.5 3.1 %copy.79 = bf16[4,4,128,512]{2,1,0,3:T(4,128)(2,1)} copy(bf16[4,4,128,512]{3,2,0,1:T(8,128)(2,1)S(1)} %all-to-all-done.2) | data formatting | bytes 4194304 | tf_op jit(solution)/shard_map/all_to_all | solution.py:87
  89.1 3.8 %all-to-all-start.3 = ((bf16[4,4,128,512]{2,1,0,3:T(4,128)(2,1)}), bf16[4,4,128,512]{2,1,0,3:T(4,128)(2,1)S(1)}, u32[]{:S(2)}, u32[]{:S(2)}) async-start(bf16[4,4,128,512]{2,1,0,3:T(4,128)(2,1)} %copy.79), calls=%async_computation.3 | async-start | bytes 4194304 | tf_op jit(solution)/shard_map/all_to_all | solution.py:86
  93.5 3.1 %fusion.10 = f32[8,16,16,256]{3,0,2,1:T(8,128)} fusion(f32[8,16,32,1]{2,0,3,1:T(8,128)S(1)} %convolution_bitcast_fusion, f32[8,16,256]{2,0,1:T(8,128)S(1)} %collective-permute-done.1, f32[16,16,256]{2,0,1:T(8,128)S(1)} %copy.87, f32[8,16,256]{2,0,1:T(8,128)S(1)} %collective-permute-done), kind=kOutput, calls=%fused_computation.19 | convolution fusion | flops 201588736 | bytes 2637824 | tf_op jit(solution)/shard_map/vzw,wyx->vzyx/dot_general | solution.py:119
  96.6 19.1 %all-to-all-done.3 = bf16[4,4,128,512]{2,1,0,3:T(4,128)(2,1)S(1)} async-done(((bf16[4,4,128,512]{2,1,0,3:T(4,128)(2,1)}), bf16[4,4,128,512]{2,1,0,3:T(4,128)(2,1)S(1)}, u32[]{:S(2)}, u32[]{:S(2)}) %all-to-all-start.3) | async-done | bytes 2097184 | tf_op jit(solution)/shard_map/all_to_all | solution.py:86
  115.8 1.8 %copy.80 = bf16[4,4,128,512]{2,3,1,0:T(8,128)(2,1)} copy(bf16[4,4,128,512]{2,1,0,3:T(4,128)(2,1)S(1)} %all-to-all-done.3) | data formatting | bytes 4194304 | tf_op jit(solution)/shard_map/all_to_all | solution.py:86
  117.6 2.8 %copy.81 = bf16[2,4,4,128,256]{4,3,2,1,0:T(8,128)(2,1)S(1)} copy(bf16[2,4,4,128,256]{3,4,0,2,1:T(8,128)(2,1)} %bitcast.98) | data formatting | bytes 4194304 | tf_op jit(solution)/shard_map/all_to_all | solution.py:86
  120.4 18.3 %scatter_custom_fusion.2 = bf16[2048,256]{1,0:T(8,128)(2,1)S(1)} fusion(s32[4096]{0:T(1024)S(1)} %bitcast.106, bf16[4096,256]{1,0:T(8,128)(2,1)S(1)} %bitcast.100, bf16[]{:T(256)} %constant.154.clone.1), kind=kCustom, calls=%fused_computation.30 | custom fusion | bytes 1048578
  140.3 2.5 %fusion.5 = f32[32,16,256]{2,0,1:T(8,128)S(1)} fusion(f32[8,16,32,1]{2,0,3,1:T(8,128)S(1)} %convolution_bitcast_fusion, f32[8,16,16,256]{3,0,2,1:T(8,128)S(1)} %copy-done.1, f32[8,16,16,256]{3,2,1,0:T(8,128)S(1)} %convert.1, f32[8]{0:T(128)S(1)} %copy-done.6), kind=kOutput, calls=%fused_computation.10 | convolution fusion | flops 202375168 | bytes 4735008 | tf_op jit(solution)/shard_map/vzw,vzyx->wyx/dot_general | solution.py:123
  146.7 4.8 %collective-permute-done.3 = f32[8,16,256]{2,0,1:T(8,128)S(1)} collective-permute-done((f32[8,16,256]{2,0,1:T(8,128)S(1)}, f32[8,16,256]{2,0,1:T(8,128)S(1)}, u32[]{:S(2)}, u32[]{:S(2)}) %collective-permute-start.3) | collective-permute-done | bytes 131104 | tf_op jit(solution)/shard_map/ppermute | solution.py:17
  151.7 2.7 %collective-permute-start.4 = (f32[8,16,256]{2,0,1:T(8,128)S(1)}, f32[8,16,256]{2,0,1:T(8,128)S(1)}, u32[]{:S(2)}, u32[]{:S(2)}) collective-permute-start(f32[8,16,256]{2,0,1:T(8,128)S(1)} %get-tuple-element.59), channel_id=1, source_target_pairs={{0,4},{4,8},{8,12},{1,5},{5,9},{9,13},{2,6},{6,10},{10,14},{3,7},{... | collective-permute-start | bytes 393224 | tf_op jit(solution)/shard_map/ppermute | solution.py:16
  157.0 4.4 %collective-permute-done.5 = f32[8,16,256]{2,0,1:T(8,128)S(1)} collective-permute-done((f32[8,16,256]{2,0,1:T(8,128)S(1)}, f32[8,16,256]{2,0,1:T(8,128)S(1)}, u32[]{:S(2)}, u32[]{:S(2)}) %collective-permute-start.5) | collective-permute-done | bytes 131104 | tf_op jit(solution)/shard_map/ppermute | solution.py:17
  161.3 1.8 %fusion.15 = f32[8,16,16,256]{3,0,2,1:T(8,128)S(1)} fusion(f32[8,16,32,1]{2,0,3,1:T(8,128)S(1)} %convolution_bitcast_fusion, f32[8,16,256]{2,0,1:T(8,128)S(1)} %collective-permute-done.5, f32[16,16,256]{2,0,1:T(8,128)S(1)} %multiply_divide_fusion.1, f32[8,16,256]{2,0,1:T(8,128)S(1)} %collective-permute-done.4), kind=kOutput, calls=%fused_computation.25 | convolution fusion | flops 201588736 | bytes 2637824 | tf_op jit(solution)/shard_map/vzw,wyx->vzyx/dot_general | solution.py:119
  163.1 2.5 %fusion.4 = f32[32,16,256]{2,0,1:T(8,128)S(1)} fusion(f32[8,16,32,1]{2,0,3,1:T(8,128)S(1)} %convolution_bitcast_fusion, f32[8,16,16,256]{3,0,2,1:T(8,128)S(1)} %fusion.15, f32[8,16,16,256]{3,2,1,0:T(8,128)S(1)} %convert.1, f32[8]{0:T(128)S(1)} %copy-done.6), kind=kOutput, calls=%fused_computation.9 | convolution fusion | flops 202375168 | bytes 4735008 | tf_op jit(solution)/shard_map/vzw,vzyx->wyx/dot_general | solution.py:123
  165.6 3.3 %collective-permute-start.6 = (f32[8,16,256]{2,0,1:T(8,128)S(1)}, f32[8,16,256]{2,0,1:T(8,128)S(1)}, u32[]{:S(2)}, u32[]{:S(2)}) collective-permute-start(f32[8,16,256]{2,0,1:T(8,128)S(1)} %get-tuple-element.56), channel_id=1, source_target_pairs={{0,4},{4,8},{8,12},{1,5},{5,9},{9,13},{2,6},{6,10},{10,14},{3,7},{... | collective-permute-start | bytes 393224 | tf_op jit(solution)/shard_map/ppermute | solution.py:16
  171.5 4.4 %collective-permute-done.7 = f32[8,16,256]{2,0,1:T(8,128)S(1)} collective-permute-done((f32[8,16,256]{2,0,1:T(8,128)S(1)}, f32[8,16,256]{2,0,1:T(8,128)S(1)}, u32[]{:S(2)}, u32[]{:S(2)}) %collective-permute-start.7) | collective-permute-done | bytes 131104 | tf_op jit(solution)/shard_map/ppermute | solution.py:17
  (84 shorter events, 20.5 us)
Async XLA Ops:
  0.0 39.3 %copy-start = (f32[8,8,17]{2,1,0:T(8,128)S(1)}, f32[8,8,17]{2,1,0:T(8,128)}, u32[]{:S(2)}) copy-start(f32[8,8,17]{2,1,0:T(8,128)} %param.18) | copy-start | bytes 13060
  14.0 14.1 %all-to-all-start = ((s32[4,4,128,2]{2,0,3,1:T(4,128)}), s32[4,4,128,2]{2,0,3,1:T(4,128)S(1)}, u32[]{:S(2)}, u32[]{:S(2)}) async-start(s32[4,4,128,2]{2,0,3,1:T(4,128)} %broadcast_in_dim.26), calls=%async_computation | async-start | bytes 32768 | tf_op jit(solution)/shard_map/all_to_all | solution.py:94
  28.1 5.2 %copy-start.2 = (f32[16,16,256]{2,1,0:T(8,128)S(1)}, f32[16,16,256]{2,1,0:T(8,128)}, u32[]{:S(2)}) copy-start(f32[16,16,256]{2,1,0:T(8,128)} %param.14) | copy-start | bytes 786436
  28.1 10.7 %copy-start.3 = (s32[8,64]{1,0:T(8,128)S(1)}, s32[8,64]{1,0:T(8,128)}, u32[]{:S(2)}) copy-start(s32[8,64]{1,0:T(8,128)} %param.17) | copy-start | bytes 6148
  28.1 53.9 %all-to-all-start.2 = ((bf16[4,4,128,512]{3,2,0,1:T(8,128)(2,1)}), bf16[4,4,128,512]{3,2,0,1:T(8,128)(2,1)S(1)}, u32[]{:S(2)}, u32[]{:S(2)}) async-start(bf16[4,4,128,512]{3,2,0,1:T(8,128)(2,1)} %copy.78), calls=%async_computation.2 | async-start | bytes 4194304 | tf_op jit(solution)/shard_map/all_to_all | solution.py:87
  33.5 60.0 %collective-permute-start = (f32[8,16,256]{2,0,1:T(8,128)S(1)}, f32[8,16,256]{2,0,1:T(8,128)S(1)}, u32[]{:S(2)}, u32[]{:S(2)}) collective-permute-start(f32[8,16,256]{2,0,1:T(8,128)S(1)} %get-tuple-element.61), channel_id=1, source_target_pairs={{0,4},{4,8},{8,12},{1,5},{5,9},{9,13},{2,6},{6,10},{10,14},{3,7},{... | collective-permute-start | bytes 393224 | tf_op jit(solution)/shard_map/ppermute | solution.py:16
  37.5 56.0 %collective-permute-start.1 = (f32[8,16,256]{2,0,1:T(8,128)S(1)}, f32[8,16,256]{2,0,1:T(8,128)S(1)}, u32[]{:S(2)}, u32[]{:S(2)}) collective-permute-start(f32[8,16,256]{2,0,1:T(8,128)S(1)} %get-tuple-element.62), channel_id=1, source_target_pairs={{4,0},{8,4},{12,8},{5,1},{9,5},{13,9},{6,2},{10,6},{14,10},{7,3},{... | collective-permute-start | bytes 393224 | tf_op jit(solution)/shard_map/ppermute | solution.py:17
  82.0 7.1 %all-to-all-start.1 = ((s32[4,4,128,2]{2,0,1,3:T(4,128)}), s32[4,4,128,2]{2,0,1,3:T(4,128)S(1)}, u32[]{:S(2)}, u32[]{:S(2)}) async-start(s32[4,4,128,2]{2,0,1,3:T(4,128)} %copy.76), calls=%async_computation.1 | async-start | bytes 32768 | tf_op jit(solution)/shard_map/all_to_all | solution.py:93
  88.6 4.6 %copy-start.5 = (s32[2]{0:T(128)S(1)}, s32[2]{0:T(128)}, u32[]{:S(2)}) copy-start(s32[2]{0:T(128)} %constant.177) | copy-start | bytes 28
  88.6 4.7 %copy-start.4 = (s32[2]{0:T(128)S(1)}, s32[2]{0:T(128)}, u32[]{:S(2)}) copy-start(s32[2]{0:T(128)} %constant.180) | copy-start | bytes 28
  89.1 26.6 %all-to-all-start.3 = ((bf16[4,4,128,512]{2,1,0,3:T(4,128)(2,1)}), bf16[4,4,128,512]{2,1,0,3:T(4,128)(2,1)S(1)}, u32[]{:S(2)}, u32[]{:S(2)}) async-start(bf16[4,4,128,512]{2,1,0,3:T(4,128)(2,1)} %copy.79), calls=%async_computation.3 | async-start | bytes 4194304 | tf_op jit(solution)/shard_map/all_to_all | solution.py:86
  120.4 18.6 %copy-start.6 = (f32[8]{0:T(128)S(1)}, f32[8]{0:T(128)}, u32[]{:S(2)}) copy-start(f32[8]{0:T(128)} %param.19) | copy-start | bytes 100
  138.8 1.6 copy-start.1
  142.9 3.8 %collective-permute-start.2 = (f32[8,16,256]{2,0,1:T(8,128)S(1)}, f32[8,16,256]{2,0,1:T(8,128)S(1)}, u32[]{:S(2)}, u32[]{:S(2)}) collective-permute-start(f32[8,16,256]{2,0,1:T(8,128)S(1)} %get-tuple-element.58), channel_id=1, source_target_pairs={{0,4},{4,8},{8,12},{1,5},{5,9},{9,13},{2,6},{6,10},{10,14},{3,7},{... | collective-permute-start | bytes 393224 | tf_op jit(solution)/shard_map/ppermute | solution.py:16
  144.6 6.9 %collective-permute-start.3 = (f32[8,16,256]{2,0,1:T(8,128)S(1)}, f32[8,16,256]{2,0,1:T(8,128)S(1)}, u32[]{:S(2)}, u32[]{:S(2)}) collective-permute-start(f32[8,16,256]{2,0,1:T(8,128)S(1)} %get-tuple-element.57), channel_id=1, source_target_pairs={{4,0},{8,4},{12,8},{5,1},{9,5},{13,9},{6,2},{10,6},{14,10},{7,3},{... | collective-permute-start | bytes 393224 | tf_op jit(solution)/shard_map/ppermute | solution.py:17
  151.7 5.2 %collective-permute-start.4 = (f32[8,16,256]{2,0,1:T(8,128)S(1)}, f32[8,16,256]{2,0,1:T(8,128)S(1)}, u32[]{:S(2)}, u32[]{:S(2)}) collective-permute-start(f32[8,16,256]{2,0,1:T(8,128)S(1)} %get-tuple-element.59), channel_id=1, source_target_pairs={{0,4},{4,8},{8,12},{1,5},{5,9},{9,13},{2,6},{6,10},{10,14},{3,7},{... | collective-permute-start | bytes 393224 | tf_op jit(solution)/shard_map/ppermute | solution.py:16
  154.5 6.9 %collective-permute-start.5 = (f32[8,16,256]{2,0,1:T(8,128)S(1)}, f32[8,16,256]{2,0,1:T(8,128)S(1)}, u32[]{:S(2)}, u32[]{:S(2)}) collective-permute-start(f32[8,16,256]{2,0,1:T(8,128)S(1)} %get-tuple-element.60), channel_id=1, source_target_pairs={{4,0},{8,4},{12,8},{5,1},{9,5},{13,9},{6,2},{10,6},{14,10},{7,3},{... | collective-permute-start | bytes 393224 | tf_op jit(solution)/shard_map/ppermute | solution.py:17
  165.6 5.8 %collective-permute-start.6 = (f32[8,16,256]{2,0,1:T(8,128)S(1)}, f32[8,16,256]{2,0,1:T(8,128)S(1)}, u32[]{:S(2)}, u32[]{:S(2)}) collective-permute-start(f32[8,16,256]{2,0,1:T(8,128)S(1)} %get-tuple-element.56), channel_id=1, source_target_pairs={{0,4},{4,8},{8,12},{1,5},{5,9},{9,13},{2,6},{6,10},{10,14},{3,7},{... | collective-permute-start | bytes 393224 | tf_op jit(solution)/shard_map/ppermute | solution.py:16
  169.0 6.9 %collective-permute-start.7 = (f32[8,16,256]{2,0,1:T(8,128)S(1)}, f32[8,16,256]{2,0,1:T(8,128)S(1)}, u32[]{:S(2)}, u32[]{:S(2)}) collective-permute-start(f32[8,16,256]{2,0,1:T(8,128)S(1)} %get-tuple-element.55), channel_id=1, source_target_pairs={{4,0},{8,4},{12,8},{5,1},{9,5},{13,9},{6,2},{10,6},{14,10},{7,3},{... | collective-permute-start | bytes 393224 | tf_op jit(solution)/shard_map/ppermute | solution.py:17
where the time goes:
time: 178 us; the launch traced here: 177 us
  waiting for transfers between devices  78.1 us (44%)
  local copies, waits for them, and re-layouts  42.9 us (24%)
  starting transfers between devices  35 us (20%)
  matrix products  10.7 us (6%)
  other arithmetic  9.61 us (5%)
    all_to_all x1, waiting for transfers between devices, shards(): lax.all_to_all(rows_four, 'blocks', split_axis=1, concat_axis=1, tiled=True)  41.8 us
    unnamed x21, local copies, waits for them, and re-layouts  30.4 us
    all_to_all x1, waiting for transfers between devices, shards(): lax.all_to_all(lax.all_to_all(rows_four, 'blocks', split_axis=1, concat_a...  19.1 us
    ppermute x4, waiting for transfers between devices, padded(): after = lax.ppermute(leading, axis, down)  13.6 us
    ppermute x4, starting transfers between devices, padded(): before = lax.ppermute(last, axis, up)  11.3 us
    all_to_all x1, starting transfers between devices, shards(): lax.all_to_all(ids_four, 'blocks', split_axis=1, concat_axis=1, tiled=True)  6.32 us
    all_to_all x1, starting transfers between devices, shards(): lax.all_to_all(rows_four, 'blocks', split_axis=1, concat_axis=1, tiled=True)  5.22 us
    ppermute x4, starting transfers between devices, padded(): after = lax.ppermute(leading, axis, down)  5.17 us
  transfers between devices with their start and end apart: 12, of which 9 were waited for; matrix products, arithmetic and copies ran while one was open for 10% of the time, Pallas kernels for 0%

commit v1 on v0

v1 whole, which is shorter than its diff:
```python
import functools

import jax
import jax.numpy as jnp
from jax import lax
from jax.experimental import pallas as pl
from jax.experimental.pallas import tpu as pltpu
from jax.sharding import PartitionSpec as P

ITERS = 2
HW = 8
CHUNKS = 4
MESH = pl.DeviceIdType.MESH
f32, bf16 = jnp.float32, jnp.bfloat16


def xor(a, b, size):
    out, bit = 0, 1
    while bit < size:
        p, q = (a // bit) % 2, (b // bit) % 2
        out = out + bit * (p + q - 2 * p * q)
        bit *= 2
    return out


def split3(value, axis):
    hi = value.astype(bf16)
    lo = (value - hi.astype(f32)).astype(bf16)
    return jnp.concatenate([hi, lo, hi], axis=axis)


def weights3(rep, width):
    hi = rep.astype(bf16)
    lo = rep - hi.astype(f32)
    lane = lax.broadcasted_iota(jnp.int32, rep.shape, 1)
    return jnp.where(lane < 2 * width, hi.astype(f32), lo).astype(bf16)


def kernel(
    nb, nv, est_in, meas, targ, f_rep, b_rep, norm, bg, out,
    packed, idsend, recv, idrecv, obs, fwd, est0, est1, share, hal, spout, spin, f3, b3,
    data_send, data_recv, id_send, id_recv, own_sem, hal_send, hal_recv,
):
    vc, lines, width = meas.shape
    rows, depth, xl = est0.shape
    cap = 2 * lines // nb
    n = nb * nv
    per = rows // CHUNKS
    my_b, my_g = lax.axis_index("blocks"), lax.axis_index("views")
    has_prev, has_next = my_b > 0, my_b < nb - 1

    def each(body):
        if n <= 16:
            for i in range(n - 1):
                body(n - 1 - i)
        else:
            def step(i, carry):
                body(n - 1 - i)
                return carry
            lax.fori_loop(0, n - 1, step, 0)

    def peer(o):
        return xor(my_b, o // nv, nb), xor(my_g, o % nv, nv)

    barrier = pltpu.get_barrier_semaphore()

    def greet(o):
        b, g = peer(o)
        pl.semaphore_signal(
            barrier, inc=1, device_id={"blocks": b, "views": g}, device_id_type=MESH
        )

    each(greet)

    idsend[...] = jnp.zeros_like(idsend)
    high = max(16, nb)
    before = (
        lax.broadcasted_iota(jnp.int32, (lines, lines), 0)
        < lax.broadcasted_iota(jnp.int32, (lines, lines), 1)
    )
    before = jnp.where(before, 1.0, 0.0).astype(bf16)
    block_of = lax.broadcasted_iota(jnp.int32, (high, lines), 0)
    slot_of = lax.broadcasted_iota(jnp.int32, (nb * cap, lines), 0).astype(f32)
    for v in range(vc):
        t = targ[v]
        inside = (t >= block_of * lines) & (t < (block_of + 1) * lines)
        member = jnp.where(inside, 1.0, 0.0)
        rank = jnp.dot(member.astype(bf16), before, preferred_element_type=f32)
        place = rank + (block_of * cap).astype(f32)
        slot = jnp.sum(member * place, axis=0, keepdims=True)
        first = jnp.sum(member * (block_of * lines).astype(f32), axis=0, keepdims=True)
        local = t - first.astype(jnp.int32)
        shift = rows.bit_length() - 1
        line = (local & (rows - 1)) * depth + (local >> shift)
        pick = jnp.where(slot_of == slot, 1.0, 0.0).astype(bf16)
        moved = jnp.dot(pick, meas[v], preferred_element_type=f32).astype(bf16)
        for b in range(nb):
            for g in range(nv):
                packed[b, g, v * cap:(v + 1) * cap, :] = moved[
                    b * cap:(b + 1) * cap, g * xl:(g + 1) * xl
                ]
        ids = jnp.broadcast_to((line + 1).astype(f32), (16, lines)).astype(bf16)
        ids = lax.dot_general(
            ids, pick, (((1,), (1,)), ((), ())), preferred_element_type=f32
        )
        for b in range(nb):
            idsend[b, v:v + 1, :cap] = ids[0:1, b * cap:(b + 1) * cap]

    for y in range(rows):
        est0[y] = est_in[:, y, :]

    pl.semaphore_wait(barrier, n - 1)

    def copies(o):
        b, g = peer(o)
        to = {"blocks": b, "views": g}
        return (
            pltpu.make_async_remote_copy(
                src_ref=packed.at[b, g], dst_ref=recv.at[o], send_sem=data_send.at[o],
                recv_sem=data_recv.at[o], device_id=to, device_id_type=MESH,
            ),
            pltpu.make_async_remote_copy(
                src_ref=idsend.at[b], dst_ref=idrecv.at[o], send_sem=id_send.at[o],
                recv_sem=id_recv.at[o], device_id=to, device_id_type=MESH,
            ),
        )

    def halo(phase, c, src_up, dst_up, src_down, dst_down):
        up = pltpu.make_async_remote_copy(
            src_ref=src_up, dst_ref=dst_up, send_sem=hal_send.at[phase, 0, c],
            recv_sem=hal_recv.at[phase, 0, c],
            device_id={"blocks": lax.rem(my_b + 1, nb)}, device_id_type=MESH,
        )
        down = pltpu.make_async_remote_copy(
            src_ref=src_down, dst_ref=dst_down, send_sem=hal_send.at[phase, 1, c],
            recv_sem=hal_recv.at[phase, 1, c],
            device_id={"blocks": lax.rem(my_b + nb - 1, nb)}, device_id_type=MESH,
        )

        def start():
            pl.when(has_next)(up.start)
            pl.when(has_prev)(down.start)

        def arrived():
            pl.when(has_prev)(up.wait_recv)
            pl.when(has_next)(down.wait_recv)

        def sent():
            pl.when(has_next)(up.wait_send)
            pl.when(has_prev)(down.wait_send)

        return start, arrived, sent

    def est_halo(sweep, c):
        if sweep == 0:
            est, ys = est0, pl.ds(0, rows)
        else:
            est, ys = est1, pl.ds(c * per, per)
        return halo(
            2 * sweep, c,
            est.at[ys, depth - HW:depth, :], hal.at[sweep, 0, ys],
            est.at[ys, 0:HW, :], hal.at[sweep, 1, ys],
        )

    def sp_halo(sweep, c):
        ys = pl.ds(c * per, per)
        return halo(
            2 * sweep + 1, c,
            spout.at[sweep, 1, ys], spin.at[sweep, 0, ys],
            spout.at[sweep, 0, ys], spin.at[sweep, 1, ys],
        )

    est_halo(0, 0)[0]()

    def send(o):
        data, ids = copies(o)
        ids.start()
        data.start()

    each(send)
    own = pltpu.make_async_copy(packed.at[my_b, my_g], recv.at[0], own_sem.at[0])
    own_id = pltpu.make_async_copy(idsend.at[my_b], idrecv.at[0], own_sem.at[1])
    own.start()
    own_id.start()

    @pl.when(my_b == 0)
    def _():
        for s in range(ITERS):
            hal[s, 0] = jnp.zeros_like(hal[s, 0])
            spin[s, 0] = jnp.zeros_like(spin[s, 0])

    @pl.when(my_b == nb - 1)
    def _():
        for s in range(ITERS):
            hal[s, 1] = jnp.zeros_like(hal[s, 1])
            spin[s, 1] = jnp.zeros_like(spin[s, 1])

    obs[...] = jnp.zeros_like(obs)
    window = depth + 2 * HW
    f3[...] = weights3(f_rep[...], window)
    b3[...] = weights3(b_rep[...], bg.shape[0])
    level = jnp.broadcast_to(bg[...], (bg.shape[0], xl))

    def project(sweep, est, y):
        field = jnp.concatenate([hal[sweep, 0, y], est[y], hal[sweep, 1, y]], axis=0)
        return jnp.dot(f3[...], split3(field, 0), preferred_element_type=f32) + level

    def loop(count, body):
        def step(i, carry):
            body(i)
            return carry
        lax.fori_loop(0, count, step, 0)

    est_halo(0, 0)[1]()

    def first_forward(c):
        for j in range(per):
            y = c * per + j
            fwd[y] = project(0, est0, y)

    loop(CHUNKS, first_forward)

    row_of = (lax.broadcasted_iota(jnp.int32, (lines, cap), 0) + 1).astype(f32)

    def put(o):
        g = xor(my_g, o % nv, nv)
        for v in range(vc):
            pick = jnp.where(idrecv[o, v:v + 1, :cap] == row_of, 1.0, 0.0).astype(bf16)
            found = jnp.dot(
                pick, recv[o, v * cap:(v + 1) * cap, :], preferred_element_type=f32
            ).reshape(rows, depth, xl)
            at = pl.ds(pl.multiple_of((g * vc + v) * depth, depth), depth)
            obs[:, at, :] = obs[:, at, :] + found

    own.wait()
    own_id.wait()
    put(0)

    def take(i):
        data, ids = copies(i)
        ids.wait_recv()
        data.wait_recv()
        put(i)

    if n <= 16:
        for o in range(1, n):
            take(o)
    else:
        loop(n - 1, lambda i: take(i + 1))

    scale = 1.0 / jnp.broadcast_to(norm[...], (depth, xl))
    for sweep in range(ITERS):
        est = est0 if sweep == 0 else est1

        def back(c):
            if sweep > 0:
                est_halo(sweep, c)[1]()
            for j in range(per):
                y = c * per + j
                forward = fwd[y] if sweep == 0 else project(sweep, est, y)
                ratio = obs[y] / forward
                spread = jnp.dot(b3[...], split3(ratio, 0), preferred_element_type=f32)
                spout[sweep, 0, y] = spread[:HW]
                share[y] = spread[HW:HW + depth]
                spout[sweep, 1, y] = spread[HW + depth:]
            sp_halo(sweep, c)[0]()

        def update(c):
            sp_halo(sweep, c)[1]()
            for j in range(per):
                y = c * per + j
                total = share[y] + jnp.concatenate(
                    [spin[sweep, 0, y], spin[sweep, 1, y]], axis=0
                )
                value = est[y] * (total * scale)
                if sweep == 0:
                    est1[y] = value
                else:
                    share[y] = value
            if sweep == 0:
                est_halo(1, c)[0]()

        loop(CHUNKS, back)
        loop(CHUNKS, update)
    for y in range(rows):
        out[:, y, :] = share[y]

    def done(o):
        data, ids = copies(o)
        ids.wait_send()
        data.wait_send()

    each(done)
    est_halo(0, 0)[2]()

    def last(c):
        sp_halo(0, c)[2]()
        est_halo(1, c)[2]()
        sp_halo(1, c)[2]()

    loop(CHUNKS, last)


def shards(nb, nv, estimate0, measured, line_target, band, psf, background):
    depth, rows, xl = estimate0.shape
    vc, _, lines, width = measured.shape
    taps, views = psf.shape[2], psf.shape[0]
    assert depth == 2 * HW and taps == 2 * HW + 1 and lines == rows * depth <= 256
    window = depth + 2 * HW
    cap = 2 * lines // nb
    n = nb * nv
    highest = lax.Precision.HIGHEST
    start = lax.axis_index("blocks") * depth
    offsets = jnp.arange(window, dtype=jnp.int32) + start - HW
    valid = (offsets >= 0) & (offsets < band.shape[1])
    padded = jnp.pad(band, ((0, 0), (HW, HW)), mode="edge")
    near = lax.dynamic_slice_in_dim(padded, start, window, 1)
    onehot = (
        (near[:, :, None] == jnp.arange(psf.shape[1], dtype=jnp.int32)) & valid[None, :, None]
    ).astype(f32)
    coef = jnp.einsum("vwb,vbk->vwk", onehot, psf, precision=highest)
    z = jnp.arange(depth, dtype=jnp.int32)
    w = jnp.arange(window, dtype=jnp.int32)
    k = jnp.arange(taps, dtype=jnp.int32)
    forward_pick = (w[None, :, None] - z[:, None, None] == k).astype(f32)
    backward_pick = (z[None, :, None] - w[:, None, None] + 2 * HW == k).astype(f32)
    norm = jnp.einsum("vwk,wck->c", coef, backward_pick, precision=highest)
    mat = jnp.einsum("vzk,zwk->vzw", coef[:, HW:HW + depth], forward_pick, precision=highest)
    mat = mat.reshape(views * depth, window)
    f_rep = jnp.concatenate([mat] * 3, axis=1)
    b_rep = jnp.concatenate([mat.T] * 3, axis=1)
    bg = jnp.repeat(background, depth)[:, None]
    vz = views * depth
    vmem = pl.BlockSpec(memory_space=pltpu.VMEM)
    dma = pltpu.SemaphoreType.DMA
    return pl.pallas_call(
        functools.partial(kernel, nb, nv),
        out_shape=jax.ShapeDtypeStruct((depth, rows, xl), f32),
        in_specs=[vmem] * 7,
        out_specs=vmem,
        scratch_shapes=[
            pltpu.VMEM((nb, nv, vc * cap, xl), bf16),
            pltpu.VMEM((nb, 8, 128), f32),
            pltpu.VMEM((n, vc * cap, xl), bf16),
            pltpu.VMEM((n, 8, 128), f32),
            pltpu.VMEM((rows, vz, xl), f32),
            pltpu.VMEM((rows, vz, xl), f32),
            pltpu.VMEM((rows, depth, xl), f32),
            pltpu.VMEM((rows, depth, xl), f32),
            pltpu.VMEM((rows, depth, xl), f32),
            pltpu.VMEM((ITERS, 2, rows, HW, xl), f32),
            pltpu.VMEM((ITERS, 2, rows, HW, xl), f32),
            pltpu.VMEM((ITERS, 2, rows, HW, xl), f32),
            pltpu.VMEM((vz, 3 * window), bf16),
            pltpu.VMEM((window, 3 * vz), bf16),
            dma((n,)),
            dma((n,)),
            dma((n,)),
            dma((n,)),
            dma((2,)),
            dma((2 * ITERS, 2, CHUNKS)),
            dma((2 * ITERS, 2, CHUNKS)),
        ],
        compiler_params=pltpu.CompilerParams(
            collective_id=0, has_side_effects=True, vmem_limit_bytes=48 << 20
        ),
    )(estimate0, measured[:, 0], line_target, f_rep, b_rep, norm[:, None], bg)


def solution(mesh):
    in_specs = (
        P(("groups", "blocks"), "sub", "views"),
        P("views", "sub", ("groups", "blocks"), None),
        P("views", "sub", ("groups", "blocks")),
        P(),
        P(),
        P(),
    )
    out_specs = P(("groups", "blocks"), "sub", "views")
    body = functools.partial(shards, mesh.shape["blocks"], mesh.shape["views"])
    return jax.shard_map(body, mesh=mesh, in_specs=in_specs, out_specs=out_specs, check_vma=False)
```

time: 178 us -> 79 us (0.44)
  waiting for transfers between devices: 78.1 us -> 0 us
  Pallas kernels: 0 us -> 73 us
  local copies, waits for them, and re-layouts: 42.9 us -> 3.8 us
  starting transfers between devices: 35 us -> 0 us
  matrix products: 10.7 us -> 0.88 us
  other arithmetic: 9.61 us -> 0.92 us
    pallas_call x0 -> x1, Pallas kernels: none -> 73 us  [shards(): pl.pallas_call(functools.partial(kernel, nb, nv), out_shape=jax.ShapeDtyp...]
    all_to_all x4 -> x0, waiting for transfers between devices: 61.5 us -> none  [the longest x1 41.8 us: shards(): lax.all_to_all(rows_four, 'blocks', split_axis=1, concat_axis=1, tiled=True)]
    unnamed x21 -> x9, local copies, waits for them, and re-layouts: 30.4 us -> 1.39 us
    all_to_all x4 -> x0, starting transfers between devices: 18.5 us -> none  [the longest x1 6.32 us: shards(): lax.all_to_all(ids_four, 'blocks', split_axis=1, concat_axis=1, tiled=True)]
    ppermute x8 -> x0, waiting for transfers between devices: 16.7 us -> none  [the longest x4 13.6 us: padded(): after = lax.ppermute(leading, axis, down)]
    ppermute x8 -> x0, starting transfers between devices: 16.4 us -> none  [the longest x4 11.3 us: padded(): before = lax.ppermute(last, axis, up)]
    dot_general x7 -> x3, matrix products: 10.7 us -> 0.88 us  [the longest x1 0.36 us: shards(): norm = jnp.einsum('vwk,wck->c', coef, backward_pick, precision=highest)]
    all_to_all x5 -> x0, local copies, waits for them, and re-layouts: 8.34 us -> none  [the longest x2 4.63 us: shards(): lax.all_to_all(lax.all_to_all(rows_four, 'blocks', split_axis=1, concat_a...]
  transfers between devices with their start and end apart: 12 -> 0, of which waited for: 9 -> 0; matrix products, arithmetic and copies ran while one was open for 10% -> 0% of each run, Pallas kernels for 0% -> 0%
where the time goes in v1:
time: 79 us; the launch traced here: 78.7 us
  Pallas kernels  73 us (92%)
  local copies, waits for them, and re-layouts  3.8 us (5%)
  other arithmetic  0.92 us (1%)
  matrix products  0.88 us (1%)
    pallas_call x1, Pallas kernels, shards(): pl.pallas_call(functools.partial(kernel, nb, nv), out_shape=jax.ShapeDtyp...  73 us

profile of v1, /device:TPU:0, one launch (start us, length us, event | category | flops | bytes accessed | tf_op | source)
XLA Modules:
  0.0 78.7 jit_solution(1839883456300146760)
XLA Ops:
  0.0 0.0 copy-start
  0.0 1.0 %slice_reduce_fusion.1 = (s32[8]{0:T(128)S(1)}, s32[8]{0:T(128)S(1)}) fusion(s32[8,64]{1,0:T(8,128)} %param.9), kind=kLoop, calls=%fused_computation.17 | loop fusion | bytes 128 | tf_op jit(solution)/shard_map/jit(_pad)/slice | solution.py:316
  1.0 0.1 reshape.54
  1.1 0.1 reshape.55
  1.2 0.8 pad_add_fusion
  1.9 0.1 constant_dynamic-slice_fusion
  2.0 0.7 broadcast_in_dim.9
  2.7 0.1 broadcast_in_dim_reshape.4.bg
  2.8 0.0 copy-done
  2.8 0.3 fusion.7
  3.1 0.1 copy.22
  3.2 0.4 convolution_bitcast_fusion.1.norm
  3.6 0.1 slice.20
  3.7 0.1 copy.17
  3.8 0.0 copy-start.2
  3.8 0.2 convolution_bitcast_fusion
  4.1 0.1 copy.19
  4.1 0.1 pad_maximum_fusion.f_rep
  4.3 0.0 copy-start.3
  4.3 0.0 copy-done.1
  4.3 0.5 copy-done.2
  4.8 0.2 copy-done.3
  5.0 73.0 %shard_map.64 = f32[16,16,256]{2,1,0:T(8,128)S(1)} custom-call(f32[16,16,256]{2,1,0:T(8,128)S(1)} %copy-done.2, bf16[4,256,512]{2,1,0:T(8,128)(2,1)S(1)} %bitcast.14, s32[4,1,256]{2,1,0:T(1,128)S(1)} %copy-done.3, f32[128,96]{1,0:T(8,128)S(1)} %pad_maximum_fusion.f_rep, f32[32,384]{1,0:T(8,128)S(1)} %pad_maximum_fusion.1.b_rep, ...), custom_call_target="tpu_custom_call" | custom-call | tf_op jit(solution)/shard_map/pallas_call | solution.py:336
  78.0 0.7 copy.24
  (6 shorter events, 0.0 us)
Async XLA Ops:
  0.0 2.8 %copy-start = (f32[8,8,17]{2,1,0:T(8,128)S(1)}, f32[8,8,17]{2,1,0:T(8,128)}, u32[]{:S(2)}) copy-start(f32[8,8,17]{2,1,0:T(8,128)} %param.10) | copy-start | bytes 13060
  0.0 4.3 %copy-start.1 = (bf16[4,1,256,512]{3,2,1,0:T(8,128)(2,1)S(1)}, bf16[4,1,256,512]{3,2,1,0:T(8,128)(2,1)}, u32[]{:S(2)}) copy-start(bf16[4,1,256,512]{3,2,1,0:T(8,128)(2,1)} %param.7) | copy-start | bytes 3145732
  3.8 1.0 %copy-start.2 = (f32[16,16,256]{2,1,0:T(8,128)S(1)}, f32[16,16,256]{2,1,0:T(8,128)}, u32[]{:S(2)}) copy-start(f32[16,16,256]{2,1,0:T(8,128)} %est_in.1) | copy-start | bytes 786436
  4.3 0.7 copy-start.3

commit v2 on v1

--- a/solution.py
+++ b/solution.py
@@ -29,16 +29,9 @@
     return jnp.concatenate([hi, lo, hi], axis=axis)
 
 
-def weights3(rep, width):
-    hi = rep.astype(bf16)
-    lo = rep - hi.astype(f32)
-    lane = lax.broadcasted_iota(jnp.int32, rep.shape, 1)
-    return jnp.where(lane < 2 * width, hi.astype(f32), lo).astype(bf16)
-
-
 def kernel(
-    nb, nv, est_in, meas, targ, f_rep, b_rep, norm, bg, out,
-    packed, idsend, recv, idrecv, obs, fwd, est0, est1, share, hal, spout, spin, f3, b3,
+    nb, nv, est_in, meas, targ, band, psf, bg, out,
+    packed, idsend, recv, idrecv, obs, fwd, est0, est1, share, hal, spout, spin, f3, b3, b3s, coefs, acc,
     data_send, data_recv, id_send, id_recv, own_sem, hal_send, hal_recv,
 ):
     vc, lines, width = meas.shape
@@ -81,7 +74,7 @@
     before = jnp.where(before, 1.0, 0.0).astype(bf16)
     block_of = lax.broadcasted_iota(jnp.int32, (high, lines), 0)
     slot_of = lax.broadcasted_iota(jnp.int32, (nb * cap, lines), 0).astype(f32)
-    for v in range(vc):
+    def pack(v):
         t = targ[v]
         inside = (t >= block_of * lines) & (t < (block_of + 1) * lines)
         member = jnp.where(inside, 1.0, 0.0)
@@ -106,23 +99,27 @@
         for b in range(nb):
             idsend[b, v:v + 1, :cap] = ids[0:1, b * cap:(b + 1) * cap]
 
+    pack(0)
     for y in range(rows):
         est0[y] = est_in[:, y, :]
 
     pl.semaphore_wait(barrier, n - 1)
 
-    def copies(o):
+    def data_copy(o, v):
         b, g = peer(o)
-        to = {"blocks": b, "views": g}
-        return (
-            pltpu.make_async_remote_copy(
-                src_ref=packed.at[b, g], dst_ref=recv.at[o], send_sem=data_send.at[o],
-                recv_sem=data_recv.at[o], device_id=to, device_id_type=MESH,
-            ),
-            pltpu.make_async_remote_copy(
-                src_ref=idsend.at[b], dst_ref=idrecv.at[o], send_sem=id_send.at[o],
-                recv_sem=id_recv.at[o], device_id=to, device_id_type=MESH,
-            ),
+        at = pl.ds(v * cap, cap)
+        return pltpu.make_async_remote_copy(
+            src_ref=packed.at[b, g, at], dst_ref=recv.at[o, at], send_sem=data_send.at[o, v],
+            recv_sem=data_recv.at[o, v], device_id={"blocks": b, "views": g},
+            device_id_type=MESH,
+        )
+
+    def id_copy(o):
+        b, g = peer(o)
+        return pltpu.make_async_remote_copy(
+            src_ref=idsend.at[b], dst_ref=idrecv.at[o], send_sem=id_send.at[o],
+            recv_sem=id_recv.at[o], device_id={"blocks": b, "views": g},
+            device_id_type=MESH,
         )
 
     def halo(phase, c, src_up, dst_up, src_down, dst_down):
@@ -170,14 +167,13 @@
             spout.at[sweep, 0, ys], spin.at[sweep, 1, ys],
         )
 
+    each(lambda o: data_copy(o, 0).start())
     est_halo(0, 0)[0]()
-
-    def send(o):
-        data, ids = copies(o)
-        ids.start()
-        data.start()
-
-    each(send)
+    for v in range(1, vc):
+        pack(v)
+        if v == vc - 1:
+            each(lambda o: id_copy(o).start())
+        each(lambda o: data_copy(o, v).start())
     own = pltpu.make_async_copy(packed.at[my_b, my_g], recv.at[0], own_sem.at[0])
     own_id = pltpu.make_async_copy(idsend.at[my_b], idrecv.at[0], own_sem.at[1])
     own.start()
@@ -197,9 +193,64 @@
 
     obs[...] = jnp.zeros_like(obs)
     window = depth + 2 * HW
-    f3[...] = weights3(f_rep[...], window)
-    b3[...] = weights3(b_rep[...], bg.shape[0])
-    level = jnp.broadcast_to(bg[...], (bg.shape[0], xl))
+    views, bands, taps = psf.shape
+    order = [g * vc + v for v in range(vc) for g in range(nv)]
+    nz = band.shape[1]
+    iota = functools.partial(lax.broadcasted_iota, jnp.int32)
+
+    in_band = jnp.concatenate(
+        [jnp.broadcast_to(band[v:v + 1, :], (bands, nz)) for v in range(views)], axis=0
+    ) == lax.rem(iota((views * bands, nz), 0), bands)
+    in_band = jnp.where(in_band, 1.0, 0.0).astype(bf16)
+    reach = iota((window, nz), 1) - iota((window, nz), 0) == my_b * depth - HW
+    reach = jnp.where(reach, 1.0, 0.0).astype(bf16)
+    near = lax.dot_general(
+        reach, in_band, (((1,), (1,)), ((), ())), preferred_element_type=f32
+    )
+    lane_view = iota(near.shape, 1) // bands
+    near = jnp.concatenate(
+        [jnp.where(lane_view == v, near, 0.0) for v in range(views)], axis=0
+    ).astype(bf16)
+    table = psf[...].reshape(views * bands, taps)
+    found = None
+    for _ in range(3):
+        part = table.astype(bf16)
+        table = table - part.astype(f32)
+        term = jnp.dot(near, part, preferred_element_type=f32)
+        found = term if found is None else found + term
+    coefs[...] = jnp.zeros_like(coefs)
+    for v in range(views):
+        coefs[v, :, :taps] = found[v * window:(v + 1) * window]
+
+    centre = jnp.concatenate([coefs[v, HW:HW + depth, :] for v in order], axis=0)
+    row_z = lax.rem(iota(centre.shape, 0), depth)
+    mat = jnp.where(row_z == 0, centre, 0.0)
+    for z in range(1, depth):
+        mat = mat + jnp.where(row_z == z, pltpu.roll(centre, z, 1), 0.0)
+    hi = mat.astype(bf16).astype(f32)
+    lo = (mat - hi).astype(bf16).astype(f32)
+    triple = hi + pltpu.roll(hi, window, 1) + pltpu.roll(lo, 2 * window, 1)
+    f3[...] = triple[:, :3 * window].astype(bf16)
+    hi_t, lo_t = hi.T[:window], lo.T[:window]
+    b3[...] = jnp.concatenate([hi_t, hi_t, lo_t], axis=1).astype(bf16)
+    part_rows = nv * depth
+    for v in range(vc):
+        at = slice(v * part_rows, (v + 1) * part_rows)
+        pad = jnp.zeros((-3 * part_rows % 128, 128), f32)
+        stack = jnp.concatenate([hi[at], hi[at], lo[at], pad], axis=0)
+        b3s[v] = stack.T[:window, :3 * part_rows].astype(bf16)
+
+    both = coefs[0]
+    for v in range(1, views):
+        both = both + coefs[v]
+    place_sum = iota(both.shape, 0) + iota(both.shape, 1)
+    norm = jnp.zeros((depth, xl), f32)
+    for z in range(depth):
+        only = jnp.where(place_sum == z + 2 * HW, both, 0.0)
+        only = jnp.sum(jnp.sum(only, axis=0, keepdims=True), axis=1, keepdims=True)
+        norm = jnp.where(iota((depth, xl), 0) == z, only, norm)
+    scale = 1.0 / norm
+    level = jnp.concatenate([jnp.full((depth, xl), bg[v], f32) for v in order], axis=0)
 
     def project(sweep, est, y):
         field = jnp.concatenate([hal[sweep, 0, y], est[y], hal[sweep, 1, y]], axis=0)
@@ -222,33 +273,39 @@
 
     row_of = (lax.broadcasted_iota(jnp.int32, (lines, cap), 0) + 1).astype(f32)
 
-    def put(o):
+    def put(o, v):
         g = xor(my_g, o % nv, nv)
-        for v in range(vc):
-            pick = jnp.where(idrecv[o, v:v + 1, :cap] == row_of, 1.0, 0.0).astype(bf16)
-            found = jnp.dot(
-                pick, recv[o, v * cap:(v + 1) * cap, :], preferred_element_type=f32
-            ).reshape(rows, depth, xl)
-            at = pl.ds(pl.multiple_of((g * vc + v) * depth, depth), depth)
-            obs[:, at, :] = obs[:, at, :] + found
+        pick = jnp.where(idrecv[o, v:v + 1, :cap] == row_of, 1.0, 0.0).astype(bf16)
+        found = jnp.dot(
+            pick, recv[o, v * cap:(v + 1) * cap, :], preferred_element_type=f32
+        ).reshape(rows, depth, xl)
+        at = pl.ds(pl.multiple_of((v * nv + g) * depth, depth), depth)
+        obs[:, at, :] = obs[:, at, :] + found
+
+    def partial_back(v, y):
+        at = slice(v * part_rows, (v + 1) * part_rows)
+        ratio = obs[y, at, :] / fwd[y, at, :]
+        part = jnp.dot(b3s[v], split3(ratio, 0), preferred_element_type=f32)
+        return part if v == 0 else acc[y] + part
 
     own.wait()
     own_id.wait()
-    put(0)
-
-    def take(i):
-        data, ids = copies(i)
-        ids.wait_recv()
-        data.wait_recv()
-        put(i)
-
-    if n <= 16:
-        for o in range(1, n):
-            take(o)
-    else:
-        loop(n - 1, lambda i: take(i + 1))
-
-    scale = 1.0 / jnp.broadcast_to(norm[...], (depth, xl))
+    for v in range(vc):
+        def take(o):
+            if v == 0:
+                id_copy(o).wait_recv()
+            data_copy(o, v).wait_recv()
+            put(o, v)
+
+        put(0, v)
+        each(take)
+        if v < vc - 1:
+            def add(c):
+                for j in range(per):
+                    acc[c * per + j] = partial_back(v, c * per + j)
+
+            loop(CHUNKS, add)
+
     for sweep in range(ITERS):
         est = est0 if sweep == 0 else est1
 
@@ -257,9 +314,11 @@
                 est_halo(sweep, c)[1]()
             for j in range(per):
                 y = c * per + j
-                forward = fwd[y] if sweep == 0 else project(sweep, est, y)
-                ratio = obs[y] / forward
-                spread = jnp.dot(b3[...], split3(ratio, 0), preferred_element_type=f32)
+                if sweep == 0:
+                    spread = partial_back(vc - 1, y)
+                else:
+                    ratio = obs[y] / project(sweep, est, y)
+                    spread = jnp.dot(b3[...], split3(ratio, 0), preferred_element_type=f32)
                 spout[sweep, 0, y] = spread[:HW]
                 share[y] = spread[HW:HW + depth]
                 spout[sweep, 1, y] = spread[HW + depth:]
@@ -286,9 +345,9 @@
         out[:, y, :] = share[y]
 
     def done(o):
-        data, ids = copies(o)
-        ids.wait_send()
-        data.wait_send()
+        id_copy(o).wait_send()
+        for v in range(vc):
+            data_copy(o, v).wait_send()
 
     each(done)
     est_halo(0, 0)[2]()
@@ -309,34 +368,14 @@
     window = depth + 2 * HW
     cap = 2 * lines // nb
     n = nb * nv
-    highest = lax.Precision.HIGHEST
-    start = lax.axis_index("blocks") * depth
-    offsets = jnp.arange(window, dtype=jnp.int32) + start - HW
-    valid = (offsets >= 0) & (offsets < band.shape[1])
-    padded = jnp.pad(band, ((0, 0), (HW, HW)), mode="edge")
-    near = lax.dynamic_slice_in_dim(padded, start, window, 1)
-    onehot = (
-        (near[:, :, None] == jnp.arange(psf.shape[1], dtype=jnp.int32)) & valid[None, :, None]
-    ).astype(f32)
-    coef = jnp.einsum("vwb,vbk->vwk", onehot, psf, precision=highest)
-    z = jnp.arange(depth, dtype=jnp.int32)
-    w = jnp.arange(window, dtype=jnp.int32)
-    k = jnp.arange(taps, dtype=jnp.int32)
-    forward_pick = (w[None, :, None] - z[:, None, None] == k).astype(f32)
-    backward_pick = (z[None, :, None] - w[:, None, None] + 2 * HW == k).astype(f32)
-    norm = jnp.einsum("vwk,wck->c", coef, backward_pick, precision=highest)
-    mat = jnp.einsum("vzk,zwk->vzw", coef[:, HW:HW + depth], forward_pick, precision=highest)
-    mat = mat.reshape(views * depth, window)
-    f_rep = jnp.concatenate([mat] * 3, axis=1)
-    b_rep = jnp.concatenate([mat.T] * 3, axis=1)
-    bg = jnp.repeat(background, depth)[:, None]
+    assert views * depth == 128 and 3 * window <= 128 and vc <= 8 and cap <= 128
     vz = views * depth
     vmem = pl.BlockSpec(memory_space=pltpu.VMEM)
     dma = pltpu.SemaphoreType.DMA
     return pl.pallas_call(
         functools.partial(kernel, nb, nv),
         out_shape=jax.ShapeDtypeStruct((depth, rows, xl), f32),
-        in_specs=[vmem] * 7,
+        in_specs=[vmem] * 5 + [pl.BlockSpec(memory_space=pltpu.SMEM)],
         out_specs=vmem,
         scratch_shapes=[
             pltpu.VMEM((nb, nv, vc * cap, xl), bf16),
@@ -353,8 +392,11 @@
             pltpu.VMEM((ITERS, 2, rows, HW, xl), f32),
             pltpu.VMEM((vz, 3 * window), bf16),
             pltpu.VMEM((window, 3 * vz), bf16),
-            dma((n,)),
-            dma((n,)),
+            pltpu.VMEM((vc, window, 3 * nv * depth), bf16),
+            pltpu.VMEM((views, window, 128), f32),
+            pltpu.VMEM((rows, window, xl), f32),
+            dma((n, vc)),
+            dma((n, vc)),
             dma((n,)),
             dma((n,)),
             dma((2,)),
@@ -364,7 +406,7 @@
         compiler_params=pltpu.CompilerParams(
             collective_id=0, has_side_effects=True, vmem_limit_bytes=48 << 20
         ),
-    )(estimate0, measured[:, 0], line_target, f_rep, b_rep, norm[:, None], bg)
+    )(estimate0, measured[:, 0], line_target, band, psf, background)
 
 
 def solution(mesh):

time: 79 us -> 79.3 us (level)
  local copies, waits for them, and re-layouts: 3.8 us -> 5.66 us
  other arithmetic: 0.92 us -> 0 us
  matrix products: 0.88 us -> 0 us
    unnamed x9 -> x13, local copies, waits for them, and re-layouts: 1.39 us -> 5.66 us
    slice x3 -> x0, local copies, waits for them, and re-layouts: 1.23 us -> none  [the longest x1 1 us: shards(): padded = jnp.pad(band, ((0, 0), (HW, HW)), mode='edge')]
    concatenate x3 -> x0, other arithmetic: 0.9 us -> none  [the longest x1 0.77 us: shards(): padded = jnp.pad(band, ((0, 0), (HW, HW)), mode='edge')]
    dot_general x3 -> x0, matrix products: 0.88 us -> none  [the longest x1 0.36 us: shards(): norm = jnp.einsum('vwk,wck->c', coef, backward_pick, precision=highest)]
where the time goes in v2:
time: 79.3 us; the launch traced here: 78.9 us
  Pallas kernels  73.3 us (92%)
  local copies, waits for them, and re-layouts  5.66 us (7%)
    pallas_call x1, Pallas kernels, shards(): pl.pallas_call(functools.partial(kernel, nb, nv), out_shape=jax.ShapeDtyp...  73.3 us
    unnamed x13, local copies, waits for them, and re-layouts  5.66 us

profile of v2, /device:TPU:0, one launch (start us, length us, event | category | flops | bytes accessed | tf_op | source)
XLA Modules:
  0.0 78.9 jit_solution(9285585861996325963)
XLA Ops:
  0.0 0.0 copy-start.5
  0.0 0.7 copy-done.5
  0.7 0.0 copy-start
  0.7 1.2 %copy-done = bf16[4,1,256,512]{3,2,1,0:T(8,128)(2,1)S(1)} copy-done((bf16[4,1,256,512]{3,2,1,0:T(8,128)(2,1)S(1)}, bf16[4,1,256,512]{3,2,1,0:T(8,128)(2,1)}, u32[]{:S(2)}) %copy-start) | copy-done | bytes 1048600
  1.9 0.0 copy-start.1
  1.9 0.9 %copy-done.1 = f32[16,16,256]{2,1,0:T(8,128)S(1)} copy-done((f32[16,16,256]{2,1,0:T(8,128)S(1)}, f32[16,16,256]{2,1,0:T(8,128)}, u32[]{:S(2)}) %copy-start.1) | copy-done | bytes 262168
  2.8 0.0 copy-start.2
  2.8 0.8 copy-done.2
  3.6 0.0 copy-start.3
  3.6 0.7 copy-done.3
  4.3 0.0 copy-start.4
  4.3 0.7 copy-done.4
  5.0 73.3 %shard_map.64 = f32[16,16,256]{2,1,0:T(8,128)S(1)} custom-call(f32[16,16,256]{2,1,0:T(8,128)S(1)} %copy-done.1, bf16[4,256,512]{2,1,0:T(8,128)(2,1)S(1)} %bitcast.1, s32[4,1,256]{2,1,0:T(1,128)S(1)} %copy-done.3, s32[8,64]{1,0:T(8,128)S(1)} %copy-done.4, f32[8,8,17]{2,1,0:T(8,128)S(1)} %copy-done.2, f32[8]{0:T(128)S(1)} %copy-done.5), custom_call_target="tpu_custom_call" | custom-call | tf_op jit(solution)/shard_map/pallas_call | solution.py:375
  78.2 0.7 copy.8
Async XLA Ops:
  0.0 0.7 copy-start.5
  0.7 1.2 %copy-start = (bf16[4,1,256,512]{3,2,1,0:T(8,128)(2,1)S(1)}, bf16[4,1,256,512]{3,2,1,0:T(8,128)(2,1)}, u32[]{:S(2)}) copy-start(bf16[4,1,256,512]{3,2,1,0:T(8,128)(2,1)} %param.7) | copy-start | bytes 3145732
  1.9 0.9 %copy-start.1 = (f32[16,16,256]{2,1,0:T(8,128)S(1)}, f32[16,16,256]{2,1,0:T(8,128)}, u32[]{:S(2)}) copy-start(f32[16,16,256]{2,1,0:T(8,128)} %est_in.1) | copy-start | bytes 786436
  2.8 0.8 copy-start.2
  3.6 0.7 copy-start.3
  4.3 0.7 copy-start.4

commit v3 on v2

--- a/solution.py
+++ b/solution.py
@@ -30,8 +30,9 @@
 
 
 def kernel(
-    nb, nv, est_in, meas, targ, band, psf, bg, out,
+    nb, nv, est_far, meas_far, targ_far, band_far, psf_far, bg, out,
     packed, idsend, recv, idrecv, obs, fwd, est0, est1, share, hal, spout, spin, f3, b3, b3s, coefs, acc,
+    est_in, meas, targ, band, psf, in_sem,
     data_send, data_recv, id_send, id_recv, own_sem, hal_send, hal_recv,
 ):
     vc, lines, width = meas.shape
@@ -44,8 +45,8 @@
 
     def each(body):
         if n <= 16:
-            for i in range(n - 1):
-                body(n - 1 - i)
+            for o in sorted(range(1, n), key=lambda o: (o < n // 2, o % nv)):
+                body(o)
         else:
             def step(i, carry):
                 body(n - 1 - i)
@@ -64,6 +65,15 @@
         )
 
     each(greet)
+    est_load, meas_load, targ_load, band_load, psf_load = [
+        pltpu.make_async_copy(source, held, in_sem.at[i])
+        for i, (source, held) in enumerate((
+            (est_far, est_in), (meas_far, meas), (targ_far, targ), (band_far, band),
+            (psf_far, psf),
+        ))
+    ]
+    for load in (targ_load, meas_load, est_load, band_load, psf_load):
+        load.start()
 
     idsend[...] = jnp.zeros_like(idsend)
     high = max(16, nb)
@@ -74,6 +84,9 @@
     before = jnp.where(before, 1.0, 0.0).astype(bf16)
     block_of = lax.broadcasted_iota(jnp.int32, (high, lines), 0)
     slot_of = lax.broadcasted_iota(jnp.int32, (nb * cap, lines), 0).astype(f32)
+    targ_load.wait()
+    meas_load.wait()
+
     def pack(v):
         t = targ[v]
         inside = (t >= block_of * lines) & (t < (block_of + 1) * lines)
@@ -100,6 +113,7 @@
             idsend[b, v:v + 1, :cap] = ids[0:1, b * cap:(b + 1) * cap]
 
     pack(0)
+    est_load.wait()
     for y in range(rows):
         est0[y] = est_in[:, y, :]
 
@@ -198,6 +212,8 @@
     nz = band.shape[1]
     iota = functools.partial(lax.broadcasted_iota, jnp.int32)
 
+    band_load.wait()
+    psf_load.wait()
     in_band = jnp.concatenate(
         [jnp.broadcast_to(band[v:v + 1, :], (bands, nz)) for v in range(views)], axis=0
     ) == lax.rem(iota((views * bands, nz), 0), bands)
@@ -375,7 +391,7 @@
     return pl.pallas_call(
         functools.partial(kernel, nb, nv),
         out_shape=jax.ShapeDtypeStruct((depth, rows, xl), f32),
-        in_specs=[vmem] * 5 + [pl.BlockSpec(memory_space=pltpu.SMEM)],
+        in_specs=[pl.BlockSpec(memory_space=pl.ANY)] * 5 + [pl.BlockSpec(memory_space=pltpu.SMEM)],
         out_specs=vmem,
         scratch_shapes=[
             pltpu.VMEM((nb, nv, vc * cap, xl), bf16),
@@ -395,6 +411,12 @@
             pltpu.VMEM((vc, window, 3 * nv * depth), bf16),
             pltpu.VMEM((views, window, 128), f32),
             pltpu.VMEM((rows, window, xl), f32),
+            pltpu.VMEM(estimate0.shape, f32),
+            pltpu.VMEM((vc, lines, width), bf16),
+            pltpu.VMEM(line_target.shape, jnp.int32),
+            pltpu.VMEM(band.shape, jnp.int32),
+            pltpu.VMEM(psf.shape, f32),
+            dma((5,)),
             dma((n, vc)),
             dma((n, vc)),
             dma((n,)),
@@ -404,7 +426,7 @@
             dma((2 * ITERS, 2, CHUNKS)),
         ],
         compiler_params=pltpu.CompilerParams(
-            collective_id=0, has_side_effects=True, vmem_limit_bytes=48 << 20
+            collective_id=0, has_side_effects=True, vmem_limit_bytes=60 << 20
         ),
     )(estimate0, measured[:, 0], line_target, band, psf, background)
 

time: 79.3 us -> 74.4 us (0.938)
  local copies, waits for them, and re-layouts: 5.66 us -> 1.67 us
    unnamed x13 -> x1, local copies, waits for them, and re-layouts: 5.66 us -> 1.67 us
where the time goes in v3:
time: 74.4 us; the launch traced here: 74.3 us
  Pallas kernels  72.6 us (98%)
  local copies, waits for them, and re-layouts  1.67 us (2%)
    pallas_call x1, Pallas kernels, shards(): pl.pallas_call(functools.partial(kernel, nb, nv), out_shape=jax.ShapeDtyp...  72.6 us
    unnamed x1, local copies, waits for them, and re-layouts  1.67 us

profile of v3, /device:TPU:0, one launch (start us, length us, event | category | flops | bytes accessed | tf_op | source)
XLA Modules:
  0.0 74.3 jit_solution(15973265593615509918)
XLA Ops:
  0.0 72.6 %shard_map.64 = f32[16,16,256]{2,1,0:T(8,128)} custom-call(f32[16,16,256]{2,1,0:T(8,128)} %est_far.1, bf16[4,256,512]{2,1,0:T(8,128)(2,1)} %bitcast.1, s32[4,1,256]{2,1,0:T(1,128)} %targ_far.1, s32[8,64]{1,0:T(8,128)} %band_far.1, f32[8,8,17]{2,1,0:T(8,128)} %psf_far.1, f32[8]{0:T(128)} %bg.1), custom_call_target="tpu_custom_call" | custom-call | tf_op jit(solution)/shard_map/pallas_call | solution.py:391
  72.6 1.7 %copy.8 = f32[16,16,256]{2,1,0:T(8,128)} copy(f32[16,16,256]{2,1,0:T(8,128)} %shard_map.64) | data formatting | bytes 524288

commit v4 on v3

--- a/solution.py
+++ b/solution.py
@@ -43,9 +43,9 @@
     my_b, my_g = lax.axis_index("blocks"), lax.axis_index("views")
     has_prev, has_next = my_b > 0, my_b < nb - 1
 
-    def each(body):
+    def each(body, near=False):
         if n <= 16:
-            for o in sorted(range(1, n), key=lambda o: (o < n // 2, o % nv)):
+            for o in sorted(range(1, n), key=lambda o: ((o < n // 2) != near, o % nv)):
                 body(o)
         else:
             def step(i, carry):
@@ -314,7 +314,7 @@
             put(o, v)
 
         put(0, v)
-        each(take)
+        each(take, near=True)
         if v < vc - 1:
             def add(c):
                 for j in range(per):

time: 74.4 us -> 73.6 us (0.989)
  Pallas kernels: 72.6 us -> 71.7 us
    pallas_call x1, Pallas kernels: 72.6 us -> 71.7 us  [shards(): pl.pallas_call(functools.partial(kernel, nb, nv), out_shape=jax.ShapeDtyp...]
where the time goes in v4:
time: 73.6 us; the launch traced here: 73.4 us
  Pallas kernels  71.7 us (97%)
  local copies, waits for them, and re-layouts  1.67 us (2%)
    pallas_call x1, Pallas kernels, shards(): pl.pallas_call(functools.partial(kernel, nb, nv), out_shape=jax.ShapeDtyp...  71.7 us
    unnamed x1, local copies, waits for them, and re-layouts  1.67 us

profile of v4, /device:TPU:0, one launch (start us, length us, event | category | flops | bytes accessed | tf_op | source)
XLA Modules:
  0.0 73.4 jit_solution(13558476512511103627)
XLA Ops:
  0.0 71.7 %shard_map.64 = f32[16,16,256]{2,1,0:T(8,128)} custom-call(f32[16,16,256]{2,1,0:T(8,128)} %est_far.1, bf16[4,256,512]{2,1,0:T(8,128)(2,1)} %bitcast.1, s32[4,1,256]{2,1,0:T(1,128)} %targ_far.1, s32[8,64]{1,0:T(8,128)} %band_far.1, f32[8,8,17]{2,1,0:T(8,128)} %psf_far.1, f32[8]{0:T(128)} %bg.1), custom_call_target="tpu_custom_call" | custom-call | tf_op jit(solution)/shard_map/pallas_call | solution.py:391
  71.8 1.7 %copy.8 = f32[16,16,256]{2,1,0:T(8,128)} copy(f32[16,16,256]{2,1,0:T(8,128)} %shard_map.64) | data formatting | bytes 524288

commit v5 on v4

--- a/solution.py
+++ b/solution.py
@@ -181,8 +181,8 @@
             spout.at[sweep, 0, ys], spin.at[sweep, 1, ys],
         )
 
+    est_halo(0, 0)[0]()
     each(lambda o: data_copy(o, 0).start())
-    est_halo(0, 0)[0]()
     for v in range(1, vc):
         pack(v)
         if v == vc - 1:

time: 73.6 us -> 73.6 us (level)
  no operation moved by 1% of the time
where the time goes in v5:
time: 73.6 us; the launch traced here: 73.4 us
  Pallas kernels  71.8 us (98%)
  local copies, waits for them, and re-layouts  1.67 us (2%)
    pallas_call x1, Pallas kernels, shards(): pl.pallas_call(functools.partial(kernel, nb, nv), out_shape=jax.ShapeDtyp...  71.8 us
    unnamed x1, local copies, waits for them, and re-layouts  1.67 us

profile of v5, /device:TPU:0, one launch (start us, length us, event | category | flops | bytes accessed | tf_op | source)
XLA Modules:
  0.0 73.4 jit_solution(3197750087358571946)
XLA Ops:
  0.0 71.8 %shard_map.64 = f32[16,16,256]{2,1,0:T(8,128)} custom-call(f32[16,16,256]{2,1,0:T(8,128)} %est_far.1, bf16[4,256,512]{2,1,0:T(8,128)(2,1)} %bitcast.1, s32[4,1,256]{2,1,0:T(1,128)} %targ_far.1, s32[8,64]{1,0:T(8,128)} %band_far.1, f32[8,8,17]{2,1,0:T(8,128)} %psf_far.1, f32[8]{0:T(128)} %bg.1), custom_call_target="tpu_custom_call" | custom-call | tf_op jit(solution)/shard_map/pallas_call | solution.py:391
  71.8 1.7 %copy.8 = f32[16,16,256]{2,1,0:T(8,128)} copy(f32[16,16,256]{2,1,0:T(8,128)} %shard_map.64) | data formatting | bytes 524288
